TPU v7x, 256 devices: a whole 4x4x8 slice. The times are simulated.
256 devices in a mesh: seq: 64 (over z, x, core), head: 4 (over y).
Axes of the slice: x: 4, y: 4, z: 8, core: 2. Of those that a mesh axis runs over, the one named last changes fastest.
Arguments:
- queries: bfloat16 [32768, 6144], P('seq', 'head'), may hold values from -6 to 6
- key_rows: bfloat16 [32768, 6144], P('seq', 'head'), may hold values from -6 to 6
- values: bfloat16 [32768, 6144], P('seq', 'head'), may hold values from -6 to 6
- gate_input: bfloat16 [32768, 6144], P('seq', 'head'), may hold values from -6 to 6
- norm_gain: float32 [6144], P('head'), may hold values from 0.1 to 1.9
- out_weight: bfloat16 [6144, 6144], P('head', 'seq'), may hold values from -0.078125 to 0.078125
Outputs:
- projected: bfloat16 [32768, 6144], P(('seq', 'head'))
All inputs are finite; a program needn't handle non-finite values.
Results may differ from a plain program's by a relative error of at most 0.02.
Values may be sent and summed in bfloat16 or wider, within the bound.
A program may use at most 192 MiB of HBM per device.

v0:
```python
import jax
import jax.numpy as jnp
from jax import lax
from jax.sharding import PartitionSpec as P

HEAD_DIM = 128
BLOCK = 512


def prefix_states(shard_total):
    devices_seq = lax.axis_size("seq")
    piece_len = shard_total.size // devices_seq
    pieces = shard_total.reshape(1, devices_seq, piece_len)
    row_ids = lax.broadcasted_iota(jnp.int32, (devices_seq, devices_seq), 0)
    col_ids = lax.broadcasted_iota(jnp.int32, (devices_seq, devices_seq), 1)
    lower = (row_ids > col_ids).astype(jnp.float32)
    summed = jnp.einsum(
        "ik,kjl->ijl",
        lower,
        lax.all_to_all(
            pieces.astype(jnp.bfloat16), "seq", split_axis=1, concat_axis=0, tiled=True
        ).astype(pieces.dtype),
        precision=lax.Precision.HIGHEST,
    )
    returned = lax.all_to_all(
        summed.astype(jnp.bfloat16), "seq", split_axis=0, concat_axis=1, tiled=True
    ).astype(summed.dtype)
    return returned.reshape(shard_total.shape)


def block_attention(query_blocks, key_blocks, value_blocks):
    causal = jnp.tril(jnp.ones((BLOCK, BLOCK), dtype=bool))

    def one_block(block):
        query_blk, key_blk, value_blk = block
        scores = jnp.einsum("thd,shd->hts", query_blk, key_blk, preferred_element_type=jnp.float32)
        weights = jnp.where(causal[None], scores, 0.0).astype(jnp.bfloat16)
        return jnp.einsum("hts,she->the", weights, value_blk, preferred_element_type=jnp.float32)

    return lax.map(one_block, (query_blocks, key_blocks, value_blocks))


def per_device(queries, key_rows, values, gate_input, norm_gain, out_weight):
    tok_rows = queries.shape[0]
    feature_width = queries.shape[1]
    heads_here = feature_width // HEAD_DIM
    block_count = tok_rows // BLOCK
    shape_four = (block_count, BLOCK, heads_here, HEAD_DIM)
    query_blocks = queries.reshape(shape_four)
    key_blocks = key_rows.reshape(shape_four)
    value_blocks = values.reshape(shape_four)
    block_states = jnp.einsum(
        "bthd,bthe->bhde", key_blocks, value_blocks, preferred_element_type=jnp.float32
    )
    shard_total = jnp.sum(block_states, axis=0)
    prefix = prefix_states(shard_total)
    intra = block_attention(query_blocks, key_blocks, value_blocks)
    running = jnp.cumsum(block_states, axis=0)
    within = jnp.concatenate([jnp.zeros_like(block_states), running[:-1]], axis=0)
    state_in = prefix[None] + within
    inter = jnp.einsum(
        "bthd,bhde->bthe",
        query_blocks.astype(jnp.float32),
        state_in,
        precision=lax.Precision.HIGHEST,
    )
    attended = inter + intra
    mean_square = jnp.mean(attended * attended, axis=-1, keepdims=True)
    gain_four = norm_gain.reshape(heads_here, HEAD_DIM)
    gated = jax.nn.silu(gate_input.reshape(shape_four).astype(jnp.float32))
    normed = (attended * lax.rsqrt(mean_square + 1e-06) * gain_four * gated).astype(jnp.bfloat16)
    normed = normed.reshape(tok_rows, feature_width)
    full_weight = lax.all_gather(out_weight, "seq", axis=1, tiled=True)
    return lax.psum_scatter(
        jnp.dot(normed, full_weight, preferred_element_type=jnp.float32).astype(jnp.bfloat16),
        "head",
        scatter_dimension=0,
        tiled=True,
    )


def solution(mesh):
    in_specs = (
        P("seq", "head"),
        P("seq", "head"),
        P("seq", "head"),
        P("seq", "head"),
        P("head"),
        P("head", "seq"),
    )
    out_specs = P(("seq", "head"), None)
    return jax.shard_map(
        per_device, mesh=mesh, in_specs=in_specs, out_specs=out_specs, check_vma=False
    )
```

profile of v0, /device:TPU:1, one launch (start us, length us, event | category | flops | bytes accessed | tf_op | source)
XLA Modules:
  0.0 211.0 jit_solution(6842223896672274669)
XLA Ops:
  6.5 0.0 all-gather.2.cloned.1.call-start
  6.5 0.7 all-gather.2.cloned.1.call-update
  7.3 1.7 copy.30
  9.0 0.0 copy-start
  9.0 2.3 %copy.31 = bf16[512,1536]{0,1:T(8,128)(2,1)S(1)} copy(bf16[512,1536]{1,0:T(8,128)(2,1)} %param.8) | data formatting | bytes 3145728 | tf_op args[2]
  11.3 0.0 copy-start.1
  11.3 0.6 convolution_convert_fusion.2
  11.9 0.0 copy-done
  11.9 1.0 convert_element_type.58
  12.9 0.5 broadcast.32
  13.4 4.7 %reduce.2 = bf16[64,3072]{1,0:T(8,128)(2,1)} reduce(bf16[64,1,3072]{2,1,0:T(2,128)(2,1)} %bitcast.37, bf16[]{:T(256)} %broadcast.32), dimensions={1}, to_apply=%bitcast.19.reduce_sub_computation | reduce | bytes 786434
  18.1 0.0 copy-start.2
  18.1 1.4 reshape.123
  19.5 0.0 copy-done.1
  19.5 31.6 %all_to_all.8 = bf16[64,2,1536]{2,1,0:T(2,128)(2,1)} all-to-all(bf16[64,2,1536]{2,1,0:T(2,128)(2,1)S(1)} %reshape.123), channel_id=1, replica_groups=mesh['seq'=64,'head'=4] {'seq'}, dimensions={0} | all-to-all | bytes 786432 | tf_op jit(solution)/shard_map/all_to_all | solution.py:20
  51.2 2.7 %reshape.124 = bf16[64,1,3072]{2,1,0:T(2,128)(2,1)S(1)} reshape(bf16[64,2,1536]{2,1,0:T(2,128)(2,1)} %all_to_all.8) | data formatting | bytes 786432
  53.9 0.3 fusion.5
  54.2 0.9 reduce.3
  55.1 1.0 reshape.125
  56.1 5.3 %all-to-all-start.1 = ((bf16[64,2,1536]{2,1,0:T(2,128)(2,1)}), bf16[64,2,1536]{2,1,0:T(2,128)(2,1)S(1)}, u32[]{:S(2)}, u32[]{:S(2)}) async-start(bf16[64,2,1536]{2,1,0:T(2,128)(2,1)} %reshape.125), calls=%async_computation.1 | async-start | bytes 786432 | tf_op jit(solution)/shard_map/all_to_all | solution.py:25
  61.4 0.2 reduce-scatter.2.cloned.1.call-start
  61.6 0.0 copy-done.2
  61.6 1.6 copy.35
  63.2 1.7 copy.40
  65.0 0.8 iota_compare_fusion
  65.7 10.8 %all-to-all-done.1 = bf16[64,2,1536]{2,1,0:T(2,128)(2,1)S(1)} async-done(((bf16[64,2,1536]{2,1,0:T(2,128)(2,1)}), bf16[64,2,1536]{2,1,0:T(2,128)(2,1)S(1)}, u32[]{:S(2)}, u32[]{:S(2)}) %all-to-all-start.1) | async-done | bytes 393248 | tf_op jit(solution)/shard_map/all_to_all | solution.py:25
  76.6 1.1 reshape.126
  77.6 4.2 %reduce.1 = bf16[64,3072]{1,0:T(8,128)(2,1)} reduce(bf16[64,1,3072]{2,1,0:T(2,128)(2,1)} %reshape.126, bf16[]{:T(256)} %constant.29), dimensions={1}, to_apply=%all_to_all.5.reduce_sub_computation | reduce | bytes 786434 | tf_op jit(solution)/shard_map/all_to_all | solution.py:25
  81.8 1.2 reshape.118
  83.0 3.7 %fusion.9 = f32[12,128,512]{2,1,0:T(8,128)} fusion(bf16[12,128,128]{2,1,0:T(8,128)(2,1)S(1)} %reshape.118, bf16[512,12,128]{0,2,1:T(8,128)(2,1)} %bitcast.35), kind=kOutput, calls=%fused_computation.18 | convolution fusion | flops 201326592 | bytes 5111808 | tf_op jit(solution)/shard_map/bthd,bhde->bthe/dot_general | solution.py:61
  86.7 0.0 copy-start.3
  86.7 9.6 %multiply_reduce_fusion = (f32[512,12]{0,1:T(8,128)S(1)}, f32[1,512,12,128]{1,3,2,0:T(8,128)}) fusion(bf16[512,12,128]{0,2,1:T(8,128)(2,1)} %bitcast.34, pred[512,512]{1,0:T(8,128)(4,1)} %iota_compare_fusion, bf16[512,12,128]{0,2,1:T(8,128)(2,1)} %bitcast.36, bf16[512,12,128]{0,2,1:T(8,128)(2,1)} %bitcast.32, f32[12,128,512]{2,1,0:T(8,128)} %fusion.9), kind=kOutput, calls=%fused_computation.10 | convolution fusion | flops 1619257344 | bytes 11296768 | tf_op jit(solution)/shard_map/while/body/eval_jaxpr/hts,she->the/dot_general | solution.py:38
  96.3 0.0 copy-done.3
  96.3 4.3 %multiply_convert_fusion = bf16[1,512,12,128]{1,3,2,0:T(8,128)(2,1)} fusion(f32[1,512,12,128]{1,3,2,0:T(8,128)S(1)} %bitcast.30, f32[1,512,12,128]{1,3,2,0:T(8,128)} %get-tuple-element.16, f32[12,128]{1,0:T(8,128)S(1)} %bitcast.40, f32[512,12]{0,1:T(8,128)S(1)} %add_rsqrt_fusion), kind=kLoop, calls=%fused_computation.9 | loop fusion | flops 6291456 | bytes 7895040 | tf_op jit(solution)/shard_map/convert_element_type | solution.py:71
  100.6 24.0 %all-gather.2.cloned.1.call-done = bf16[1536,6144]{0,1:T(8,128)(2,1)} async-done(((bf16[1536,96]{0,1:T(8,128)(2,1)}), bf16[1536,6144]{0,1:T(8,128)(2,1)}) %all-gather.2.cloned.1.call-update) | async-done | bytes 18874384 | tf_op jit(solution)/shard_map/all_gather | solution.py:73
  124.6 16.0 %convolution_convert_fusion = bf16[512,6144]{1,0:T(8,128)(2,1)} fusion(bf16[512,1536]{0,1:T(8,128)(2,1)} %bitcast.39, bf16[1536,6144]{0,1:T(8,128)(2,1)} %all-gather.2.cloned.1.call-done), kind=kOutput, calls=%fused_computation.1 | convolution fusion | flops 9666822144 | bytes 26738688 | tf_op jit(solution)/shard_map/dot_general | solution.py:75
  140.6 0.0 reduce-scatter.2.cloned.1.call-update
  140.7 63.5 %reduce-scatter.2.cloned.1.call-done = bf16[128,6144]{1,0:T(8,128)(2,1)} async-done(((bf16[512,6144]{1,0:T(8,128)(2,1)}), bf16[128,6144]{1,0:T(8,128)(2,1)}) %reduce-scatter.2.cloned.1.call-update) | async-done | bytes 1572880 | tf_op jit(solution)/shard_map/reduce_scatter | solution.py:74
  (1 shorter events, 0.0 us)
Async XLA Ops:
  6.5 118.1 %all-gather.2.cloned.1.call-start = ((), (), s32[]{:S(2)}) async-start(), calls=%async_computation.3 | async-start | bytes 19169280 | tf_op jit(solution)/shard_map/all_gather | solution.py:73
  9.0 2.9 %copy-start = (bf16[512,1536]{0,1:T(8,128)(2,1)}, bf16[512,1536]{0,1:T(8,128)(2,1)S(1)}, u32[]{:S(2)}) copy-start(bf16[512,1536]{0,1:T(8,128)(2,1)S(1)} %copy.30) | copy-start | bytes 4718596
  11.3 8.2 %copy-start.1 = (bf16[512,1536]{0,1:T(8,128)(2,1)}, bf16[512,1536]{0,1:T(8,128)(2,1)S(1)}, u32[]{:S(2)}) copy-start(bf16[512,1536]{0,1:T(8,128)(2,1)S(1)} %copy.31) | copy-start | bytes 4718596
  18.1 43.5 %copy-start.2 = (bf16[512,1536]{1,0:T(8,128)(2,1)S(1)}, bf16[512,1536]{1,0:T(8,128)(2,1)}, u32[]{:S(2)}) copy-start(bf16[512,1536]{1,0:T(8,128)(2,1)} %param.6) | copy-start | bytes 4718596
  56.1 20.5 %all-to-all-start.1 = ((bf16[64,2,1536]{2,1,0:T(2,128)(2,1)}), bf16[64,2,1536]{2,1,0:T(2,128)(2,1)S(1)}, u32[]{:S(2)}, u32[]{:S(2)}) async-start(bf16[64,2,1536]{2,1,0:T(2,128)(2,1)} %reshape.125), calls=%async_computation.1 | async-start | bytes 786432 | tf_op jit(solution)/shard_map/all_to_all | solution.py:25
  61.4 142.8 %reduce-scatter.2.cloned.1.call-start = ((), (), s32[]{:S(2)}) async-start(), calls=%async_computation.4 | async-start | bytes 7864320 | tf_op jit(solution)/shard_map/reduce_scatter | solution.py:74
  86.7 9.6 %copy-start.3 = (f32[1536]{0:T(1024)S(1)}, f32[1536]{0:T(1024)}, u32[]{:S(2)}) copy-start(f32[1536]{0:T(1024)} %param.10) | copy-start | bytes 18436
Sparse Core Ops, SparseCore 0:
  10.1 114.4 all-gather.1
  140.8 63.3 reduce-scatter.1
where the time goes:
time: 212 us; the launch traced here: 211 us
  waiting for transfers between devices  99.1 us (47%)
  blocking collectives  31.6 us (15%)
  matrix products  30.1 us (14%)
  local copies, waits for them, and re-layouts  16.3 us (8%)
  other arithmetic  14.8 us (7%)
  between operations  13.5 us (6%)
  starting transfers between devices  5.52 us (3%)
    reduce_scatter x1, waiting for transfers between devices, per_device(): lax.psum_scatter(jnp.dot(normed, full_weight, preferred_element_type=jnp....  63.5 us
    all_to_all x1, blocking collectives, prefix_states(): lax.all_to_all(pieces.astype(jnp.bfloat16), 'seq', split_axis=1, concat_a...  31.6 us
    all_gather x1, waiting for transfers between devices, per_device(): full_weight = lax.all_gather(out_weight, 'seq', axis=1, tiled=True)  24 us
    dot_general x1, matrix products, per_device(): jnp.dot(normed, full_weight, preferred_element_type=jnp.float32)  16 us
    unnamed x16, local copies, waits for them, and re-layouts  12.4 us
    all_to_all x1, waiting for transfers between devices, prefix_states(): lax.all_to_all(summed.astype(jnp.bfloat16), 'seq', split_axis=0, concat_a...  10.8 us
    dot_general x1, matrix products, one_block(): jnp.einsum('hts,she->the', weights, value_blk, preferred_element_type=jnp...  9.56 us
    all_to_all x1, starting transfers between devices, prefix_states(): lax.all_to_all(summed.astype(jnp.bfloat16), 'seq', split_axis=0, concat_a...  5.3 us
  transfers between devices with their start and end apart: 3, of which 3 were waited for; matrix products, arithmetic and copies ran while one was open for 21% of the time, Pallas kernels for 0%

commit v1 on v0

v1 whole, which is shorter than its diff:
```python
import functools

import jax
import jax.numpy as jnp
from jax import lax
from jax.experimental import pallas as pl
from jax.experimental.pallas import tpu as pltpu
from jax.sharding import PartitionSpec as P

HD = 128
NZ, NX, NC, NY = 8, 4, 2, 4
NP = NX * NC
TOK = 512
WID = 1536
HEADS = WID // HD
SH = 96
PLANE = NP * SH
D = NZ * PLANE
QT = TOK // NY
PIECE = WID // NP
SUB = PIECE // NZ
HALF = SH // 2
HC = PLANE // 2
F32, BF16 = jnp.float32, jnp.bfloat16
NT = (((1,), (1,)), ((), ()))
TN = (((0,), (0,)), ((), ()))


def kernel(
    q_hbm, k_hbm, v_hbm, g_hbm, gain_ref, w_hbm, o_hbm,
    qb, kb, vb, gb, wraw, wt, st, sin, intra, gate, nrm,
    pr1, pr3, zt, za, zb, zp, pf, t1, t2, r1, r2, ob,
    ld, out_sem, zs, zr, xs, xr, ss, sr, p1s, p1r, p2s, p2r, p3s, p3r, p4s, p4r, ys, yr,
):
    s = lax.axis_index("seq")
    h = lax.axis_index("head")
    c = lax.rem(s, NC)
    x = lax.rem(s // NC, NX)
    z = s // NP
    p = lax.rem(s, NP)

    def at_zx(zz, xx, cc):
        return (zz * NX + xx) * NC + cc

    zu, zd = lax.rem(z + 1, NZ), lax.rem(z + NZ - 1, NZ)
    xu, xd = lax.rem(x + 1, NX), lax.rem(x + NX - 1, NX)
    hu, hd, h2 = lax.rem(h + 1, NY), lax.rem(h + NY - 1, NY), lax.rem(h + 2, NY)
    dev_zu, dev_zd = at_zx(zu, x, c), at_zx(zd, x, c)
    dev_xu, dev_xd = at_zx(z, xu, c), at_zx(z, xd, c)
    dev_sib = at_zx(z, x, 1 - c)

    sends = []

    def remote(src, dst, send_sem, recv_sem, seq=s, head=h):
        return pltpu.make_async_remote_copy(
            src_ref=src, dst_ref=dst, send_sem=send_sem, recv_sem=recv_sem,
            device_id=(seq, head), device_id_type=pl.DeviceIdType.MESH,
        )

    def send(*args, **kw):
        cp = remote(*args, **kw)
        cp.start()
        sends.append(cp)

    def arrive(dst, recv_sem):
        remote(dst, dst, recv_sem, recv_sem, seq=dev_sib).wait_recv()

    def plane(j):
        off = -(j + 1) // 2 if j % 2 else j // 2
        return lax.rem(z + off + NZ, NZ)

    loads = [
        pltpu.make_async_copy(src, dst, ld.at[i])
        for i, (src, dst) in enumerate(
            ((k_hbm, kb), (v_hbm, vb), (w_hbm, wraw), (q_hbm, qb), (g_hbm, gb))
        )
    ]
    for cp in loads:
        cp.start()

    bar = pltpu.get_barrier_semaphore()
    for i in range(1, NP):
        pl.semaphore_signal(bar, inc=1, device_id=(z * NP + lax.rem(p + i, NP), h), device_id_type=pl.DeviceIdType.MESH)
    for i in range(1, NZ):
        pl.semaphore_signal(bar, inc=1, device_id=(lax.rem(z + i, NZ) * NP + p, h), device_id_type=pl.DeviceIdType.MESH)
    for hh in (hu, hd):
        pl.semaphore_signal(bar, inc=1, device_id=(s, hh), device_id_type=pl.DeviceIdType.MESH)

    def shard(pln, xx, cc):
        return wt.at[pln, xx, cc]

    def z_start():
        own = shard(z, x, c)
        send(own, own, zs.at[0], zr.at[1], seq=dev_zu)
        send(own, own, zs.at[1], zr.at[2], seq=dev_zd)

    def z_recv(j):
        ref = shard(plane(j), x, c)
        if j == 7:
            arrive(ref.at[pl.ds(0, HALF)], zr.at[7])
            arrive(ref.at[pl.ds(HALF, HALF)], zr.at[8])
            return
        arrive(ref, zr.at[j])
        to = dev_zu if j % 2 else dev_zd
        if j == 5:
            ref = ref.at[pl.ds(0, HALF)]
        if j == 6:
            ref = ref.at[pl.ds(HALF, HALF)]
        send(ref, ref, zs.at[j + 1], zr.at[j + 2], seq=to)

    def x_start(j):
        ref = shard(plane(j), x, c)
        send(ref, ref, xs.at[j, 0], xr.at[j, 0], seq=dev_xu)
        send(ref, ref, xs.at[j, 1], xr.at[j, 1], seq=dev_xd)

    def x_forward(j):
        pln = plane(j)
        ref = shard(pln, xd, c)
        arrive(ref, xr.at[j, 0])
        ref = ref.at[pl.ds(0, HALF)]
        send(ref, ref, xs.at[j, 2], xr.at[j, 2], seq=dev_xu)
        ref = shard(pln, xu, c)
        arrive(ref, xr.at[j, 1])
        ref = ref.at[pl.ds(HALF, HALF)]
        send(ref, ref, xs.at[j, 3], xr.at[j, 3], seq=dev_xd)

    def sib_start(j):
        pln = plane(j)
        ref = shard(pln, lax.rem(x + 2, NX), c)
        arrive(ref.at[pl.ds(0, HALF)], xr.at[j, 2])
        arrive(ref.at[pl.ds(HALF, HALF)], xr.at[j, 3])
        for i in range(NX):
            ref = shard(pln, i, c)
            send(ref, ref, ss.at[j, i], sr.at[j, i], seq=dev_sib)

    def sib_recv(j):
        pln = plane(j)
        for i in range(NX):
            arrive(shard(pln, i, 1 - c), sr.at[j, i])

    with jax.named_scope("local_state"):
        loads[0].wait()
        loads[1].wait()

        def one_state(i, carry):
            cols = pl.ds(pl.multiple_of(i * HD, HD), HD)
            st[cols, :] = lax.dot_general(kb[:, cols], vb[:, cols], TN, preferred_element_type=F32).astype(BF16)
            return carry

        lax.fori_loop(0, HEADS, one_state, 0)

    with jax.named_scope("entry_barrier"):
        pl.semaphore_wait(bar, NP - 1 + NZ - 1 + 2)

    def piece_rows(i):
        return pl.ds(pl.multiple_of(i * PIECE, PIECE), PIECE)

    with jax.named_scope("plane_send"):
        for i in range(1, NP):
            to = lax.rem(p + i, NP)
            send(st.at[piece_rows(to)], pr1.at[p], p1s.at[i], p1r.at[i], seq=z * NP + to)
        pr1[p] = st[piece_rows(p), :]

    with jax.named_scope("weight_transpose"):
        loads[2].wait()
        eye = (lax.broadcasted_iota(jnp.int32, (SH, SH), 0) == lax.broadcasted_iota(jnp.int32, (SH, SH), 1)).astype(BF16)
        wt[z, x, c] = lax.dot_general(eye, wraw[...], NT, preferred_element_type=F32).astype(BF16)
        z_start()

    loads[3].wait()
    HB = TOK // 2
    tri = lax.broadcasted_iota(jnp.int32, (HB, HB), 0) >= lax.broadcasted_iota(jnp.int32, (HB, HB), 1)

    def one_intra(i, carry):
        cols = pl.ds(pl.multiple_of(i * HD, HD), HD)
        lo, hi = pl.ds(0, HB), pl.ds(HB, HB)
        v_lo = vb[lo, cols]
        sc = lax.dot_general(qb[lo, cols], kb[lo, cols], NT, preferred_element_type=F32)
        sc = jnp.where(tri, sc, 0.0).astype(BF16)
        intra[lo, cols] = jnp.dot(sc, v_lo, preferred_element_type=F32)
        sa = lax.dot_general(qb[hi, cols], kb[lo, cols], NT, preferred_element_type=F32).astype(BF16)
        sd = lax.dot_general(qb[hi, cols], kb[hi, cols], NT, preferred_element_type=F32)
        sd = jnp.where(tri, sd, 0.0).astype(BF16)
        intra[hi, cols] = jnp.dot(sa, v_lo, preferred_element_type=F32) + jnp.dot(sd, vb[hi, cols], preferred_element_type=F32)
        return carry

    def one_gate(i, carry):
        cols = pl.ds(pl.multiple_of(i * HD, HD), HD)
        gi = gb[:, cols].astype(F32)
        gate[:, cols] = gi / (1.0 + jnp.exp(-gi)) * gain_ref[:, cols]
        return carry

    with jax.named_scope("intra_a"):
        lax.fori_loop(0, HEADS // 2, one_intra, 0)

    def sub_rows(i):
        return pl.ds(pl.multiple_of(i * SUB, SUB), SUB)

    with jax.named_scope("plane_recv"):
        for i in range(1, NP):
            arrive(pr1.at[lax.rem(p + NP - i, NP)], p1r.at[i])
        total = pr1[0].astype(F32)
        for i in range(1, NP):
            total = total + pr1[i].astype(F32)
        zt[...] = total
        for i in range(1, NZ):
            to = lax.rem(z + i, NZ)
            send(zt.at[sub_rows(to)], za.at[z], p2s.at[i], p2r.at[i], seq=to * NP + p)
        za[z] = zt[sub_rows(z), :]
        x_start(0)

    with jax.named_scope("intra_b"):
        lax.fori_loop(HEADS // 2, HEADS, one_intra, 0)

    with jax.named_scope("z_scan"):
        for i in range(1, NZ):
            arrive(za.at[lax.rem(z + NZ - i, NZ)], p2r.at[i])
        run = jnp.zeros((SUB, HD), F32)
        for i in range(NZ):
            zb[i] = run
            run = run + za[i]
        for i in range(1, NZ):
            to = lax.rem(z + i, NZ)
            send(zb.at[to], zp.at[sub_rows(z)], p3s.at[i], p3r.at[i], seq=to * NP + p)
        zp[sub_rows(z), :] = zb[z]

    with jax.named_scope("gate"):
        loads[4].wait()
        lax.fori_loop(0, HEADS, one_gate, 0)

    with jax.named_scope("z_back"):
        for i in range(1, NZ):
            arrive(zp.at[sub_rows(lax.rem(z + NZ - i, NZ))], p3r.at[i])
        run = zp[...]
        for i in range(NP):
            pr3[i] = run.astype(BF16)
            run = run + pr1[i].astype(F32)
        for i in range(1, NP):
            to = lax.rem(p + i, NP)
            send(pr3.at[to], sin.at[piece_rows(p)], p4s.at[i], p4r.at[i], seq=z * NP + to)
        sin[piece_rows(p), :] = pr3[p]

    with jax.named_scope("gather_early"):
        x_forward(0)
        z_recv(1)
        z_recv(2)
        x_start(1)
        z_recv(3)
        z_recv(4)
        sib_start(0)

    with jax.named_scope("state_recv"):
        for i in range(1, NP):
            arrive(sin.at[piece_rows(lax.rem(p + NP - i, NP))], p4r.at[i])

    def one_head(i, carry):
        cols = pl.ds(pl.multiple_of(i * HD, HD), HD)
        att = intra[:, cols] + jnp.dot(qb[:, cols], sin[cols, :], preferred_element_type=F32)
        ms = jnp.mean(att * att, axis=-1, keepdims=True)
        nrm[:, cols] = (att * lax.rsqrt(ms + 1e-06) * gate[:, cols]).astype(BF16)
        return carry

    with jax.named_scope("attend"):
        lax.fori_loop(0, HEADS, one_head, 0)

    def q_rows(i):
        return pl.ds(pl.multiple_of(i * QT, QT), QT)

    def project(j):
        pln = plane(j)
        for i in range(NX):
            w = wt[pln, i].reshape(NC * SH, WID)
            pf[j % 3, :, pl.ds(i * NC * SH, NC * SH)] = lax.dot_general(nrm[...], w, NT, preferred_element_type=F32)

    def rs_first(j):
        t1[j, 0] = pf[j % 3, q_rows(h2), pl.ds(0, HC)].astype(BF16)
        t1[j, 1] = pf[j % 3, q_rows(h2), pl.ds(HC, HC)].astype(BF16)
        send(t1.at[j, 0], r1.at[j, 0], ys.at[j, 0], yr.at[j, 0], head=hu)
        send(t1.at[j, 1], r1.at[j, 1], ys.at[j, 1], yr.at[j, 1], head=hd)

    def rs_second(j):
        a = j % 3
        t2[j, 0, :, pl.ds(HC, HC)] = pf[a, q_rows(hu), pl.ds(HC, HC)].astype(BF16)
        t2[j, 1, :, pl.ds(0, HC)] = pf[a, q_rows(hd), pl.ds(0, HC)].astype(BF16)
        arrive(r1.at[j, 0], yr.at[j, 0])
        t2[j, 0, :, pl.ds(0, HC)] = (pf[a, q_rows(hu), pl.ds(0, HC)] + r1[j, 0].astype(F32)).astype(BF16)
        send(t2.at[j, 0], r2.at[j, 0], ys.at[j, 2], yr.at[j, 2], head=hu)
        arrive(r1.at[j, 1], yr.at[j, 1])
        t2[j, 1, :, pl.ds(HC, HC)] = (pf[a, q_rows(hd), pl.ds(HC, HC)] + r1[j, 1].astype(F32)).astype(BF16)
        send(t2.at[j, 1], r2.at[j, 1], ys.at[j, 3], yr.at[j, 3], head=hd)

    outs = []

    def rs_last(j):
        arrive(r2.at[j, 0], yr.at[j, 2])
        arrive(r2.at[j, 1], yr.at[j, 3])
        ob[j] = (pf[j % 3, q_rows(h), :] + r2[j, 0].astype(F32) + r2[j, 1].astype(F32)).astype(BF16)
        cols = pl.ds(pl.multiple_of(plane(j) * PLANE, PLANE), PLANE)
        cp = pltpu.make_async_copy(ob.at[j], o_hbm.at[:, cols], out_sem.at[j])
        cp.start()
        outs.append(cp)

    for j in range(NZ + 2):
        if j < NZ:
            with jax.named_scope(f"plane_wait_{j}"):
                sib_recv(j)
            with jax.named_scope(f"project_{j}"):
                project(j)
                rs_first(j)
        if j + 1 < NZ:
            with jax.named_scope(f"gather_{j}"):
                x_forward(j + 1)
                if j + 2 < NZ:
                    x_start(j + 2)
                if j == 0:
                    z_recv(5)
                    z_recv(6)
                if j == 1:
                    z_recv(7)
        if 1 <= j <= NZ:
            with jax.named_scope(f"reduce_{j}"):
                rs_second(j - 1)
        if j + 1 < NZ:
            with jax.named_scope(f"sibling_{j}"):
                sib_start(j + 1)
        if j >= 2:
            with jax.named_scope(f"finish_{j}"):
                rs_last(j - 2)

    with jax.named_scope("drain"):
        for cp in outs:
            cp.wait()
        for cp in sends:
            cp.wait_send()


def per_device(queries, key_rows, values, gate_input, norm_gain, out_weight):
    anyspec = pl.BlockSpec(memory_space=pl.ANY)
    dma = lambda *n: pltpu.SemaphoreType.DMA(n)
    return pl.pallas_call(
        kernel,
        out_shape=jax.ShapeDtypeStruct((QT, D), BF16),
        in_specs=[anyspec] * 4 + [pl.BlockSpec(memory_space=pltpu.VMEM), anyspec],
        out_specs=anyspec,
        scratch_shapes=[
            pltpu.VMEM((TOK, WID), BF16),
            pltpu.VMEM((TOK, WID), BF16),
            pltpu.VMEM((TOK, WID), BF16),
            pltpu.VMEM((TOK, WID), BF16),
            pltpu.VMEM((WID, SH), BF16),
            pltpu.VMEM((NZ, NX, NC, SH, WID), BF16),
            pltpu.VMEM((WID, HD), BF16),
            pltpu.VMEM((WID, HD), BF16),
            pltpu.VMEM((TOK, WID), F32),
            pltpu.VMEM((TOK, WID), F32),
            pltpu.VMEM((TOK, WID), BF16),
            pltpu.VMEM((NP, PIECE, HD), BF16),
            pltpu.VMEM((NP, PIECE, HD), BF16),
            pltpu.VMEM((PIECE, HD), F32),
            pltpu.VMEM((NZ, SUB, HD), F32),
            pltpu.VMEM((NZ, SUB, HD), F32),
            pltpu.VMEM((PIECE, HD), F32),
            pltpu.VMEM((3, TOK, PLANE), F32),
            pltpu.VMEM((NZ, 2, QT, HC), BF16),
            pltpu.VMEM((NZ, 2, QT, PLANE), BF16),
            pltpu.VMEM((NZ, 2, QT, HC), BF16),
            pltpu.VMEM((NZ, 2, QT, PLANE), BF16),
            pltpu.VMEM((NZ, QT, PLANE), BF16),
            dma(5), dma(NZ),
            dma(9), dma(9),
            dma(NZ, 4), dma(NZ, 4),
            dma(NZ, NX), dma(NZ, NX),
            dma(NP), dma(NP), dma(NZ), dma(NZ), dma(NZ), dma(NZ), dma(NP), dma(NP),
            dma(NZ, 4), dma(NZ, 4),
        ],
        compiler_params=pltpu.CompilerParams(
            collective_id=0, has_side_effects=True, vmem_limit_bytes=60 * 1024 * 1024
        ),
    )(queries, key_rows, values, gate_input, norm_gain.reshape(1, WID), out_weight)


def solution(mesh):
    in_specs = (
        P("seq", "head"),
        P("seq", "head"),
        P("seq", "head"),
        P("seq", "head"),
        P("head"),
        P("head", "seq"),
    )
    return jax.shard_map(
        per_device,
        mesh=mesh,
        in_specs=in_specs,
        out_specs=P(("seq", "head"), None),
        check_vma=False,
    )
```

time: 212 us -> 146 us (0.69)
  Pallas kernels: 0 us -> 140 us
  waiting for transfers between devices: 99.1 us -> 0 us
  blocking collectives: 31.6 us -> 0 us
  matrix products: 30.1 us -> 0 us
  other arithmetic: 14.8 us -> 0 us
  between operations: 13.5 us -> 0.01 us
  local copies, waits for them, and re-layouts: 16.3 us -> 5.86 us
  starting transfers between devices: 5.52 us -> 0 us
    pallas_call x0 -> x1, Pallas kernels: none -> 140 us  [per_device(): pl.pallas_call(kernel, out_shape=jax.ShapeDtypeStruct((QT, D), BF16), in_...]
    reduce_scatter x1 -> x0, waiting for transfers between devices: 63.5 us -> none  [per_device(): lax.psum_scatter(jnp.dot(normed, full_weight, preferred_element_type=jnp....]
    all_to_all x1 -> x0, blocking collectives: 31.6 us -> none  [prefix_states(): lax.all_to_all(pieces.astype(jnp.bfloat16), 'seq', split_axis=1, concat_a...]
    dot_general x5 -> x0, matrix products: 30.1 us -> none  [the longest x1 16 us: per_device(): jnp.dot(normed, full_weight, preferred_element_type=jnp.float32)]
    all_gather x1 -> x0, waiting for transfers between devices: 24 us -> none  [per_device(): full_weight = lax.all_gather(out_weight, 'seq', axis=1, tiled=True)]
    all_to_all x1 -> x0, waiting for transfers between devices: 10.8 us -> none  [prefix_states(): lax.all_to_all(summed.astype(jnp.bfloat16), 'seq', split_axis=0, concat_a...]
    unnamed x16 -> x2, local copies, waits for them, and re-layouts: 12.4 us -> 4.57 us
    all_to_all x1 -> x0, starting transfers between devices: 5.3 us -> none  [prefix_states(): lax.all_to_all(summed.astype(jnp.bfloat16), 'seq', split_axis=0, concat_a...]
  transfers between devices with their start and end apart: 3 -> 0, of which waited for: 3 -> 0; matrix products, arithmetic and copies ran while one was open for 21% -> 0% of each run, Pallas kernels for 0% -> 0%
where the time goes in v1:
time: 146 us
  Pallas kernels  140 us (96%)
  local copies, waits for them, and re-layouts  5.86 us (4%)
    pallas_call x1, Pallas kernels, per_device(): pl.pallas_call(kernel, out_shape=jax.ShapeDtypeStruct((QT, D), BF16), in_...  140 us
    unnamed x2, local copies, waits for them, and re-layouts  4.57 us

profile of v1, /device:TPU:1, one launch (start us, length us, event | category | flops | bytes accessed | tf_op | source)
XLA Modules:
  0.0 146.0 jit_solution(4855115566195539947)
XLA Ops:
  0.0 1.3 reshape.3.gain_ref
  1.3 1.9 %copy.7.w_hbm = bf16[1536,96]{1,0:T(8,128)(2,1)} copy(bf16[1536,96]{0,1:T(8,128)(2,1)} %param.11) | data formatting | bytes 589824 | tf_op args[5]
  3.2 140.1 %shard_map.64 = bf16[128,6144]{1,0:T(8,128)(2,1)} custom-call(bf16[512,1536]{1,0:T(8,128)(2,1)} %q_hbm.1, bf16[512,1536]{1,0:T(8,128)(2,1)} %k_hbm.1, bf16[512,1536]{1,0:T(8,128)(2,1)} %v_hbm.1, bf16[512,1536]{1,0:T(8,128)(2,1)} %g_hbm.1, f32[1,1536]{1,0:T(1,128)} %reshape.3.gain_ref, bf16[1536,96]{1,0:T(8,128)(2,1)} %copy.7.w_hbm), custom_call_target="tpu_custom_call" | custom-call | tf_op jit(solution)/shard_map/pallas_call | solution.py:340
  143.3 2.7 %copy.9 = bf16[128,6144]{1,0:T(8,128)(2,1)} copy(bf16[128,6144]{1,0:T(8,128)(2,1)} %shard_map.64) | data formatting | bytes 3145728

commit v2 on v1

--- a/solution.py
+++ b/solution.py
@@ -20,17 +20,43 @@
 PIECE = WID // NP
 SUB = PIECE // NZ
 HALF = SH // 2
-HC = PLANE // 2
+PARTS = 2
+SPLIT = 8
+NCH = NZ * PARTS
+CW = PLANE // PARTS
+QH = QT // 2
 F32, BF16 = jnp.float32, jnp.bfloat16
+KINDS = "BAABBBBA"
+ORDER = (0, 4, 1, 2, 6, 3, 5, 7)
+PLAN = {
+    "intra_a": "O0",
+    "plane_recv": "X0",
+    "intra_b": "Z2 Z1",
+    "z_sum": "F0",
+    "gate": "Z4 X4",
+    "z_back": "S0 A0",
+    "back_sum": "Z3",
+    "state_recv": "F4 Z6 X6",
+    "chunk_1": "S4 X3",
+    "after_2": "S1 F6",
+    "after_4": "Z5 S2 X5",
+    "after_5": "F3",
+    "after_6": "S6",
+    "chunk_7": "Z7 A6",
+    "after_7": "F5",
+    "after_8": "S3",
+    "after_9": "S5 A5",
+    "after_12": "S7",
+}
 NT = (((1,), (1,)), ((), ()))
 TN = (((0,), (0,)), ((), ()))
 
 
 def kernel(
     q_hbm, k_hbm, v_hbm, g_hbm, gain_ref, w_hbm, o_hbm,
-    qb, kb, vb, gb, wraw, wt, st, sin, intra, gate, nrm,
+    qb, kb, vb, gb, wt, st, sin, intra, gate, nrm,
     pr1, pr3, zt, za, zb, zp, pf, t1, t2, r1, r2, ob,
-    ld, out_sem, zs, zr, xs, xr, ss, sr, p1s, p1r, p2s, p2r, p3s, p3r, p4s, p4r, ys, yr,
+    ld, out_sem, zs, zr, xs, xr, fs, fr, ss, sr, p1s, p1r, p2s, p2r, p3s, p3r, p4s, p4r, ys, yr,
 ):
     s = lax.axis_index("seq")
     h = lax.axis_index("head")
@@ -72,7 +98,7 @@
     loads = [
         pltpu.make_async_copy(src, dst, ld.at[i])
         for i, (src, dst) in enumerate(
-            ((k_hbm, kb), (v_hbm, vb), (w_hbm, wraw), (q_hbm, qb), (g_hbm, gb))
+            ((k_hbm, kb), (v_hbm, vb), (w_hbm, wt.at[z, x, c]), (q_hbm, qb), (g_hbm, gb))
         )
     ]
     for cp in loads:
@@ -108,10 +134,15 @@
             ref = ref.at[pl.ds(HALF, HALF)]
         send(ref, ref, zs.at[j + 1], zr.at[j + 2], seq=to)
 
+    def sib_send(j, i):
+        ref = shard(plane(j), lax.rem(x + i, NX), c)
+        send(ref, ref, ss.at[j, i], sr.at[j, i], seq=dev_sib)
+
     def x_start(j):
         ref = shard(plane(j), x, c)
         send(ref, ref, xs.at[j, 0], xr.at[j, 0], seq=dev_xu)
         send(ref, ref, xs.at[j, 1], xr.at[j, 1], seq=dev_xd)
+        sib_send(j, 0)
 
     def x_forward(j):
         pln = plane(j)
@@ -119,24 +150,55 @@
         arrive(ref, xr.at[j, 0])
         ref = ref.at[pl.ds(0, HALF)]
         send(ref, ref, xs.at[j, 2], xr.at[j, 2], seq=dev_xu)
+        sib_send(j, NX - 1)
         ref = shard(pln, xu, c)
         arrive(ref, xr.at[j, 1])
         ref = ref.at[pl.ds(HALF, HALF)]
         send(ref, ref, xs.at[j, 3], xr.at[j, 3], seq=dev_xd)
-
-    def sib_start(j):
+        sib_send(j, 1)
+
+    def halves(ref):
+        return ref.at[pl.ds(0, HALF)], ref.at[pl.ds(HALF, HALF)]
+
+    def whole_start(j):
+        for i in range(1, NX):
+            ref = shard(plane(j), lax.rem(x + i, NX), c)
+            if j % 2 or j == 0:
+                up = halves(ref)[0] if j == 5 else ref
+                send(up, up, fs.at[j + 2 - (j == 0), i], fr.at[j + 2 - (j == 0), i], seq=dev_zu)
+            if j % 2 == 0:
+                dn = halves(ref)[1] if j == 6 else ref
+                send(dn, dn, fs.at[j + 2, i], fr.at[j + 2, i], seq=dev_zd)
+
+    def fill(j):
         pln = plane(j)
-        ref = shard(pln, lax.rem(x + 2, NX), c)
-        arrive(ref.at[pl.ds(0, HALF)], xr.at[j, 2])
-        arrive(ref.at[pl.ds(HALF, HALF)], xr.at[j, 3])
+        if KINDS[j] == "B":
+            lo, hi = halves(shard(pln, lax.rem(x + 2, NX), c))
+            arrive(lo, xr.at[j, 2])
+            arrive(hi, xr.at[j, 3])
+            sib_send(j, 2)
+            return
+        sib_send(j, 0)
+        for i in range(1, NX):
+            ref = shard(pln, lax.rem(x + i, NX), c)
+            if j == 7:
+                lo, hi = halves(ref)
+                arrive(lo, fr.at[7, i])
+                arrive(hi, fr.at[8, i])
+            else:
+                arrive(ref, fr.at[j, i])
+            sib_send(j, i)
+
+    def sib_recv(j):
         for i in range(NX):
-            ref = shard(pln, i, c)
-            send(ref, ref, ss.at[j, i], sr.at[j, i], seq=dev_sib)
-
-    def sib_recv(j):
-        pln = plane(j)
-        for i in range(NX):
-            arrive(shard(pln, i, 1 - c), sr.at[j, i])
+            arrive(shard(plane(j), lax.rem(x + i, NX), 1 - c), sr.at[j, i])
+
+    stages = {"O": lambda j: z_start(), "Z": z_recv, "X": x_start, "F": x_forward, "A": whole_start, "S": fill}
+
+    def gather(at):
+        for name in PLAN.get(at, "").split():
+            with jax.named_scope(f"gather_{name}"):
+                stages[name[0]](int(name[1]))
 
     with jax.named_scope("local_state"):
         loads[0].wait()
@@ -161,11 +223,9 @@
             send(st.at[piece_rows(to)], pr1.at[p], p1s.at[i], p1r.at[i], seq=z * NP + to)
         pr1[p] = st[piece_rows(p), :]
 
-    with jax.named_scope("weight_transpose"):
+    with jax.named_scope("weight_send"):
         loads[2].wait()
-        eye = (lax.broadcasted_iota(jnp.int32, (SH, SH), 0) == lax.broadcasted_iota(jnp.int32, (SH, SH), 1)).astype(BF16)
-        wt[z, x, c] = lax.dot_general(eye, wraw[...], NT, preferred_element_type=F32).astype(BF16)
-        z_start()
+        gather("intra_a")
 
     loads[3].wait()
     HB = TOK // 2
@@ -187,18 +247,20 @@
     def one_gate(i, carry):
         cols = pl.ds(pl.multiple_of(i * HD, HD), HD)
         gi = gb[:, cols].astype(F32)
-        gate[:, cols] = gi / (1.0 + jnp.exp(-gi)) * gain_ref[:, cols]
+        gate[:, cols] = gi / (1.0 + jnp.exp(-gi)) * gain_ref[cols].reshape(1, HD)
         return carry
 
     with jax.named_scope("intra_a"):
-        lax.fori_loop(0, HEADS // 2, one_intra, 0)
+        lax.fori_loop(0, SPLIT, one_intra, 0)
 
     def sub_rows(i):
         return pl.ds(pl.multiple_of(i * SUB, SUB), SUB)
 
+    gather("plane_recv")
     with jax.named_scope("plane_recv"):
         for i in range(1, NP):
             arrive(pr1.at[lax.rem(p + NP - i, NP)], p1r.at[i])
+        gather("plane_sum")
         total = pr1[0].astype(F32)
         for i in range(1, NP):
             total = total + pr1[i].astype(F32)
@@ -207,14 +269,16 @@
             to = lax.rem(z + i, NZ)
             send(zt.at[sub_rows(to)], za.at[z], p2s.at[i], p2r.at[i], seq=to * NP + p)
         za[z] = zt[sub_rows(z), :]
-        x_start(0)
-
+
+    gather("intra_b")
     with jax.named_scope("intra_b"):
-        lax.fori_loop(HEADS // 2, HEADS, one_intra, 0)
-
+        lax.fori_loop(SPLIT, HEADS, one_intra, 0)
+
+    gather("z_scan")
     with jax.named_scope("z_scan"):
         for i in range(1, NZ):
             arrive(za.at[lax.rem(z + NZ - i, NZ)], p2r.at[i])
+        gather("z_sum")
         run = jnp.zeros((SUB, HD), F32)
         for i in range(NZ):
             zb[i] = run
@@ -224,13 +288,16 @@
             send(zb.at[to], zp.at[sub_rows(z)], p3s.at[i], p3r.at[i], seq=to * NP + p)
         zp[sub_rows(z), :] = zb[z]
 
+    gather("gate")
     with jax.named_scope("gate"):
         loads[4].wait()
         lax.fori_loop(0, HEADS, one_gate, 0)
 
+    gather("z_back")
     with jax.named_scope("z_back"):
         for i in range(1, NZ):
             arrive(zp.at[sub_rows(lax.rem(z + NZ - i, NZ))], p3r.at[i])
+        gather("back_sum")
         run = zp[...]
         for i in range(NP):
             pr3[i] = run.astype(BF16)
@@ -240,15 +307,7 @@
             send(pr3.at[to], sin.at[piece_rows(p)], p4s.at[i], p4r.at[i], seq=z * NP + to)
         sin[piece_rows(p), :] = pr3[p]
 
-    with jax.named_scope("gather_early"):
-        x_forward(0)
-        z_recv(1)
-        z_recv(2)
-        x_start(1)
-        z_recv(3)
-        z_recv(4)
-        sib_start(0)
-
+    gather("state_recv")
     with jax.named_scope("state_recv"):
         for i in range(1, NP):
             arrive(sin.at[piece_rows(lax.rem(p + NP - i, NP))], p4r.at[i])
@@ -260,77 +319,69 @@
         nrm[:, cols] = (att * lax.rsqrt(ms + 1e-06) * gate[:, cols]).astype(BF16)
         return carry
 
+    gather("attend")
     with jax.named_scope("attend"):
         lax.fori_loop(0, HEADS, one_head, 0)
 
     def q_rows(i):
         return pl.ds(pl.multiple_of(i * QT, QT), QT)
 
-    def project(j):
-        pln = plane(j)
-        for i in range(NX):
-            w = wt[pln, i].reshape(NC * SH, WID)
-            pf[j % 3, :, pl.ds(i * NC * SH, NC * SH)] = lax.dot_general(nrm[...], w, NT, preferred_element_type=F32)
-
-    def rs_first(j):
-        t1[j, 0] = pf[j % 3, q_rows(h2), pl.ds(0, HC)].astype(BF16)
-        t1[j, 1] = pf[j % 3, q_rows(h2), pl.ds(HC, HC)].astype(BF16)
-        send(t1.at[j, 0], r1.at[j, 0], ys.at[j, 0], yr.at[j, 0], head=hu)
-        send(t1.at[j, 1], r1.at[j, 1], ys.at[j, 1], yr.at[j, 1], head=hd)
-
-    def rs_second(j):
-        a = j % 3
-        t2[j, 0, :, pl.ds(HC, HC)] = pf[a, q_rows(hu), pl.ds(HC, HC)].astype(BF16)
-        t2[j, 1, :, pl.ds(0, HC)] = pf[a, q_rows(hd), pl.ds(0, HC)].astype(BF16)
-        arrive(r1.at[j, 0], yr.at[j, 0])
-        t2[j, 0, :, pl.ds(0, HC)] = (pf[a, q_rows(hu), pl.ds(0, HC)] + r1[j, 0].astype(F32)).astype(BF16)
-        send(t2.at[j, 0], r2.at[j, 0], ys.at[j, 2], yr.at[j, 2], head=hu)
-        arrive(r1.at[j, 1], yr.at[j, 1])
-        t2[j, 1, :, pl.ds(HC, HC)] = (pf[a, q_rows(hd), pl.ds(HC, HC)] + r1[j, 1].astype(F32)).astype(BF16)
-        send(t2.at[j, 1], r2.at[j, 1], ys.at[j, 3], yr.at[j, 3], head=hd)
+    def project(n):
+        w = wt[plane(ORDER[n // PARTS]), pl.ds(n % PARTS * (NX // PARTS), NX // PARTS)].reshape(CW, WID)
+        pf[n % 3] = lax.dot_general(nrm[...], w, NT, preferred_element_type=F32)
+
+    def half_rows(i, half):
+        return pl.ds(pl.multiple_of(i * QT + half * QH, QH), QH)
+
+    def rs_first(n):
+        for half, to in ((0, hu), (1, hd)):
+            t1[n, half] = pf[n % 3, half_rows(h2, half), :].astype(BF16)
+            send(t1.at[n, half], r1.at[n, half], ys.at[n, half], yr.at[n, half], head=to)
+
+    def rs_second(n):
+        for half, to in ((0, hu), (1, hd)):
+            same, other = pl.ds(half * QH, QH), pl.ds((1 - half) * QH, QH)
+            t2[n, half, other, :] = pf[n % 3, half_rows(to, 1 - half), :].astype(BF16)
+            arrive(r1.at[n, half], yr.at[n, half])
+            t2[n, half, same, :] = (pf[n % 3, half_rows(to, half), :] + r1[n, half].astype(F32)).astype(BF16)
+            send(t2.at[n, half], r2.at[n, half], ys.at[n, 2 + half], yr.at[n, 2 + half], head=to)
 
     outs = []
 
-    def rs_last(j):
-        arrive(r2.at[j, 0], yr.at[j, 2])
-        arrive(r2.at[j, 1], yr.at[j, 3])
-        ob[j] = (pf[j % 3, q_rows(h), :] + r2[j, 0].astype(F32) + r2[j, 1].astype(F32)).astype(BF16)
-        cols = pl.ds(pl.multiple_of(plane(j) * PLANE, PLANE), PLANE)
-        cp = pltpu.make_async_copy(ob.at[j], o_hbm.at[:, cols], out_sem.at[j])
+    def rs_last(n):
+        arrive(r2.at[n, 0], yr.at[n, 2])
+        arrive(r2.at[n, 1], yr.at[n, 3])
+        ob[n] = (pf[n % 3, q_rows(h), :] + r2[n, 0].astype(F32) + r2[n, 1].astype(F32)).astype(BF16)
+        first = plane(ORDER[n // PARTS]) * PLANE + n % PARTS * CW
+        cp = pltpu.make_async_copy(ob.at[n], o_hbm.at[:, pl.ds(pl.multiple_of(first, CW), CW)], out_sem.at[n])
         cp.start()
         outs.append(cp)
 
-    for j in range(NZ + 2):
-        if j < NZ:
-            with jax.named_scope(f"plane_wait_{j}"):
-                sib_recv(j)
-            with jax.named_scope(f"project_{j}"):
-                project(j)
-                rs_first(j)
-        if j + 1 < NZ:
-            with jax.named_scope(f"gather_{j}"):
-                x_forward(j + 1)
-                if j + 2 < NZ:
-                    x_start(j + 2)
-                if j == 0:
-                    z_recv(5)
-                    z_recv(6)
-                if j == 1:
-                    z_recv(7)
-        if 1 <= j <= NZ:
-            with jax.named_scope(f"reduce_{j}"):
-                rs_second(j - 1)
-        if j + 1 < NZ:
-            with jax.named_scope(f"sibling_{j}"):
-                sib_start(j + 1)
-        if j >= 2:
-            with jax.named_scope(f"finish_{j}"):
-                rs_last(j - 2)
+    marks = [0]
+    for n in range(NCH + 2):
+        gather(f"chunk_{n}")
+        if n < NCH:
+            if n % PARTS == 0:
+                with jax.named_scope(f"plane_wait_{n}"):
+                    sib_recv(ORDER[n // PARTS])
+            with jax.named_scope(f"project_{n}"):
+                project(n)
+                rs_first(n)
+        if 1 <= n <= NCH:
+            with jax.named_scope(f"reduce_{n}"):
+                rs_second(n - 1)
+        gather(f"after_{n}")
+        if n >= 2:
+            with jax.named_scope(f"finish_{n}"):
+                for cp in sends[marks[max(0, n - 5)] : marks[max(0, n - 4)]]:
+                    cp.wait_send()
+                rs_last(n - 2)
+        marks.append(len(sends))
 
     with jax.named_scope("drain"):
         for cp in outs:
             cp.wait()
-        for cp in sends:
+        for cp in sends[marks[max(0, NCH + 1 - 4)] :]:
             cp.wait_send()
 
 
@@ -347,7 +398,6 @@
             pltpu.VMEM((TOK, WID), BF16),
             pltpu.VMEM((TOK, WID), BF16),
             pltpu.VMEM((TOK, WID), BF16),
-            pltpu.VMEM((WID, SH), BF16),
             pltpu.VMEM((NZ, NX, NC, SH, WID), BF16),
             pltpu.VMEM((WID, HD), BF16),
             pltpu.VMEM((WID, HD), BF16),
@@ -360,23 +410,24 @@
             pltpu.VMEM((NZ, SUB, HD), F32),
             pltpu.VMEM((NZ, SUB, HD), F32),
             pltpu.VMEM((PIECE, HD), F32),
-            pltpu.VMEM((3, TOK, PLANE), F32),
-            pltpu.VMEM((NZ, 2, QT, HC), BF16),
-            pltpu.VMEM((NZ, 2, QT, PLANE), BF16),
-            pltpu.VMEM((NZ, 2, QT, HC), BF16),
-            pltpu.VMEM((NZ, 2, QT, PLANE), BF16),
-            pltpu.VMEM((NZ, QT, PLANE), BF16),
-            dma(5), dma(NZ),
+            pltpu.VMEM((3, TOK, CW), F32),
+            pltpu.VMEM((NCH, 2, QH, CW), BF16),
+            pltpu.VMEM((NCH, 2, QT, CW), BF16),
+            pltpu.VMEM((NCH, 2, QH, CW), BF16),
+            pltpu.VMEM((NCH, 2, QT, CW), BF16),
+            pltpu.VMEM((NCH, QT, CW), BF16),
+            dma(5), dma(NCH),
             dma(9), dma(9),
             dma(NZ, 4), dma(NZ, 4),
+            dma(9, NX), dma(9, NX),
             dma(NZ, NX), dma(NZ, NX),
             dma(NP), dma(NP), dma(NZ), dma(NZ), dma(NZ), dma(NZ), dma(NP), dma(NP),
-            dma(NZ, 4), dma(NZ, 4),
+            dma(NCH, 4), dma(NCH, 4),
         ],
         compiler_params=pltpu.CompilerParams(
             collective_id=0, has_side_effects=True, vmem_limit_bytes=60 * 1024 * 1024
         ),
-    )(queries, key_rows, values, gate_input, norm_gain.reshape(1, WID), out_weight)
+    )(queries, key_rows, values, gate_input, norm_gain, out_weight.T)
 
 
 def solution(mesh):

time: 146 us -> 112 us (0.77)
  the two profiles are of different devices: /device:TPU:1 before, /device:TPU:104 now
where the time goes in v2:
time: 112 us; the launch traced here: 111 us
  Pallas kernels  109 us (97%)
  local copies, waits for them, and re-layouts  2.69 us (2%)
    pallas_call x1, Pallas kernels, per_device(): pl.pallas_call(kernel, out_shape=jax.ShapeDtypeStruct((QT, D), BF16), in_...  109 us
    unnamed x1, local copies, waits for them, and re-layouts  2.69 us

profile of v2, /device:TPU:104, one launch (start us, length us, event | category | flops | bytes accessed | tf_op | source)
XLA Modules:
  0.0 111.4 jit_solution(8376550432232825569)
XLA Ops:
  0.0 108.7 %shard_map.64 = bf16[128,6144]{1,0:T(8,128)(2,1)} custom-call(bf16[512,1536]{1,0:T(8,128)(2,1)} %q_hbm.1, bf16[512,1536]{1,0:T(8,128)(2,1)} %k_hbm.1, bf16[512,1536]{1,0:T(8,128)(2,1)} %v_hbm.1, bf16[512,1536]{1,0:T(8,128)(2,1)} %g_hbm.1, f32[1536]{0:T(1024)} %gain_ref.1, bf16[96,1536]{1,0:T(8,128)(2,1)} %bitcast.1), custom_call_target="tpu_custom_call" | custom-call | tf_op jit(solution)/shard_map/pallas_call | solution.py:391
  108.7 2.7 %copy.8 = bf16[128,6144]{1,0:T(8,128)(2,1)} copy(bf16[128,6144]{1,0:T(8,128)(2,1)} %shard_map.64) | data formatting | bytes 3145728

commit v3 on v2

--- a/solution.py
+++ b/solution.py
@@ -20,33 +20,35 @@
 PIECE = WID // NP
 SUB = PIECE // NZ
 HALF = SH // 2
+LAG2, LAG3 = 2, 4
+SLOTS = LAG3 + 1
 PARTS = 2
-SPLIT = 8
 NCH = NZ * PARTS
 CW = PLANE // PARTS
 QH = QT // 2
 F32, BF16 = jnp.float32, jnp.bfloat16
-KINDS = "BAABBBBA"
+KINDS = "BAABBBBB"
 ORDER = (0, 4, 1, 2, 6, 3, 5, 7)
 PLAN = {
-    "intra_a": "O0",
-    "plane_recv": "X0",
-    "intra_b": "Z2 Z1",
-    "z_sum": "F0",
-    "gate": "Z4 X4",
-    "z_back": "S0 A0",
-    "back_sum": "Z3",
-    "state_recv": "F4 Z6 X6",
-    "chunk_1": "S4 X3",
-    "after_2": "S1 F6",
-    "after_4": "Z5 S2 X5",
-    "after_5": "F3",
-    "after_6": "S6",
-    "chunk_7": "Z7 A6",
-    "after_7": "F5",
-    "after_8": "S3",
-    "after_9": "S5 A5",
-    "after_12": "S7",
+    "plane_recv": "O0 I0 Z4 X0",
+    "z_scan": "Z2 I2 Z5 G0 Z3 F0 I3 Z8",
+    "z_back": "Z9 X4 S0 A0 Z7",
+    "state_recv": "Z6 Z12 Z13 I1 F4 X6",
+    "project_1": "S4",
+    "reduce_2": "X3",
+    "reduce_3": "S1",
+    "reduce_4": "S2 F6",
+    "reduce_5": "F3",
+    "project_6": "Z11",
+    "reduce_6": "Z10",
+    "project_7": "X5",
+    "reduce_7": "S6 S3",
+    "finish_8": "F5",
+    "project_9": "Z14",
+    "project_10": "X7",
+    "finish_10": "S5",
+    "project_12": "F7",
+    "finish_13": "S7",
 }
 NT = (((1,), (1,)), ((), ()))
 TN = (((0,), (0,)), ((), ()))
@@ -115,24 +117,29 @@
     def shard(pln, xx, cc):
         return wt.at[pln, xx, cc]
 
+    def part(ref, half):
+        return ref.at[pl.ds(half * HALF, HALF)]
+
     def z_start():
         own = shard(z, x, c)
-        send(own, own, zs.at[0], zr.at[1], seq=dev_zu)
-        send(own, own, zs.at[1], zr.at[2], seq=dev_zd)
-
-    def z_recv(j):
+        for i in range(2):
+            up, dn = part(own, i), part(own, 1 - i)
+            send(up, up, zs.at[1, i], zr.at[1, i], seq=dev_zu)
+            send(dn, dn, zs.at[2, i], zr.at[2, i], seq=dev_zd)
+
+    def z_recv(j, i):
         ref = shard(plane(j), x, c)
         if j == 7:
-            arrive(ref.at[pl.ds(0, HALF)], zr.at[7])
-            arrive(ref.at[pl.ds(HALF, HALF)], zr.at[8])
+            arrive(part(ref, 0), zr.at[7, 0])
+            arrive(part(ref, 1), zr.at[7, 1])
             return
-        arrive(ref, zr.at[j])
+        ref = part(ref, i if j % 2 else 1 - i)
+        arrive(ref, zr.at[j, i])
         to = dev_zu if j % 2 else dev_zd
-        if j == 5:
-            ref = ref.at[pl.ds(0, HALF)]
-        if j == 6:
-            ref = ref.at[pl.ds(HALF, HALF)]
-        send(ref, ref, zs.at[j + 1], zr.at[j + 2], seq=to)
+        if j < 5:
+            send(ref, ref, zs.at[j + 2, i], zr.at[j + 2, i], seq=to)
+        elif i == 0:
+            send(ref, ref, zs.at[7, j - 5], zr.at[7, j - 5], seq=to)
 
     def sib_send(j, i):
         ref = shard(plane(j), lax.rem(x + i, NX), c)
@@ -140,25 +147,23 @@
 
     def x_start(j):
         ref = shard(plane(j), x, c)
-        send(ref, ref, xs.at[j, 0], xr.at[j, 0], seq=dev_xu)
-        send(ref, ref, xs.at[j, 1], xr.at[j, 1], seq=dev_xd)
+        for i in range(2):
+            up, dn = part(ref, i), part(ref, 1 - i)
+            send(up, up, xs.at[j, i], xr.at[j, i], seq=dev_xu)
+            send(dn, dn, xs.at[j, 2 + i], xr.at[j, 2 + i], seq=dev_xd)
         sib_send(j, 0)
 
     def x_forward(j):
         pln = plane(j)
-        ref = shard(pln, xd, c)
+        ref = part(shard(pln, xd, c), 0)
         arrive(ref, xr.at[j, 0])
-        ref = ref.at[pl.ds(0, HALF)]
-        send(ref, ref, xs.at[j, 2], xr.at[j, 2], seq=dev_xu)
-        sib_send(j, NX - 1)
-        ref = shard(pln, xu, c)
-        arrive(ref, xr.at[j, 1])
-        ref = ref.at[pl.ds(HALF, HALF)]
-        send(ref, ref, xs.at[j, 3], xr.at[j, 3], seq=dev_xd)
-        sib_send(j, 1)
+        send(ref, ref, xs.at[j, 4], xr.at[j, 4], seq=dev_xu)
+        ref = part(shard(pln, xu, c), 1)
+        arrive(ref, xr.at[j, 2])
+        send(ref, ref, xs.at[j, 5], xr.at[j, 5], seq=dev_xd)
 
     def halves(ref):
-        return ref.at[pl.ds(0, HALF)], ref.at[pl.ds(HALF, HALF)]
+        return part(ref, 0), part(ref, 1)
 
     def whole_start(j):
         for i in range(1, NX):
@@ -174,8 +179,12 @@
         pln = plane(j)
         if KINDS[j] == "B":
             lo, hi = halves(shard(pln, lax.rem(x + 2, NX), c))
-            arrive(lo, xr.at[j, 2])
-            arrive(hi, xr.at[j, 3])
+            arrive(part(shard(pln, xd, c), 1), xr.at[j, 1])
+            sib_send(j, 3)
+            arrive(part(shard(pln, xu, c), 0), xr.at[j, 3])
+            sib_send(j, 1)
+            arrive(lo, xr.at[j, 4])
+            arrive(hi, xr.at[j, 5])
             sib_send(j, 2)
             return
         sib_send(j, 0)
@@ -193,12 +202,12 @@
         for i in range(NX):
             arrive(shard(plane(j), lax.rem(x + i, NX), 1 - c), sr.at[j, i])
 
-    stages = {"O": lambda j: z_start(), "Z": z_recv, "X": x_start, "F": x_forward, "A": whole_start, "S": fill}
+    stages = {"O": lambda j: z_start(), "Z": lambda j: z_recv(j // 2, j % 2), "X": x_start, "F": x_forward, "A": whole_start, "S": fill}
 
     def gather(at):
         for name in PLAN.get(at, "").split():
             with jax.named_scope(f"gather_{name}"):
-                stages[name[0]](int(name[1]))
+                stages[name[0]](int(name[1:]))
 
     with jax.named_scope("local_state"):
         loads[0].wait()
@@ -223,26 +232,26 @@
             send(st.at[piece_rows(to)], pr1.at[p], p1s.at[i], p1r.at[i], seq=z * NP + to)
         pr1[p] = st[piece_rows(p), :]
 
-    with jax.named_scope("weight_send"):
+    with jax.named_scope("weight_load"):
         loads[2].wait()
-        gather("intra_a")
-
-    loads[3].wait()
+        loads[3].wait()
+        loads[4].wait()
+
     HB = TOK // 2
     tri = lax.broadcasted_iota(jnp.int32, (HB, HB), 0) >= lax.broadcasted_iota(jnp.int32, (HB, HB), 1)
 
-    def one_intra(i, carry):
-        cols = pl.ds(pl.multiple_of(i * HD, HD), HD)
+    def some_intra(first):
         lo, hi = pl.ds(0, HB), pl.ds(HB, HB)
-        v_lo = vb[lo, cols]
-        sc = lax.dot_general(qb[lo, cols], kb[lo, cols], NT, preferred_element_type=F32)
-        sc = jnp.where(tri, sc, 0.0).astype(BF16)
-        intra[lo, cols] = jnp.dot(sc, v_lo, preferred_element_type=F32)
-        sa = lax.dot_general(qb[hi, cols], kb[lo, cols], NT, preferred_element_type=F32).astype(BF16)
-        sd = lax.dot_general(qb[hi, cols], kb[hi, cols], NT, preferred_element_type=F32)
-        sd = jnp.where(tri, sd, 0.0).astype(BF16)
-        intra[hi, cols] = jnp.dot(sa, v_lo, preferred_element_type=F32) + jnp.dot(sd, vb[hi, cols], preferred_element_type=F32)
-        return carry
+        cols = [pl.ds((first + k) * HD, HD) for k in range(3)]
+        low = [lax.dot_general(qb[lo, cl], kb[lo, cl], NT, preferred_element_type=F32) for cl in cols]
+        low = [jnp.where(tri, a, 0.0).astype(BF16) for a in low]
+        for cl, a in zip(cols, low):
+            intra[lo, cl] = jnp.dot(a, vb[lo, cl], preferred_element_type=F32)
+        full = [lax.dot_general(qb[hi, cl], kb[lo, cl], NT, preferred_element_type=F32).astype(BF16) for cl in cols]
+        diag = [lax.dot_general(qb[hi, cl], kb[hi, cl], NT, preferred_element_type=F32) for cl in cols]
+        diag = [jnp.where(tri, a, 0.0).astype(BF16) for a in diag]
+        for cl, a, d in zip(cols, full, diag):
+            intra[hi, cl] = jnp.dot(a, vb[lo, cl], preferred_element_type=F32) + jnp.dot(d, vb[hi, cl], preferred_element_type=F32)
 
     def one_gate(i, carry):
         cols = pl.ds(pl.multiple_of(i * HD, HD), HD)
@@ -250,17 +259,19 @@
         gate[:, cols] = gi / (1.0 + jnp.exp(-gi)) * gain_ref[cols].reshape(1, HD)
         return carry
 
-    with jax.named_scope("intra_a"):
-        lax.fori_loop(0, SPLIT, one_intra, 0)
+    def intra_part(i):
+        some_intra(3 * i)
+
+    stages["I"] = intra_part
+    stages["G"] = lambda j: lax.fori_loop(0, HEADS, one_gate, 0)
+    gather("plane_recv")
 
     def sub_rows(i):
         return pl.ds(pl.multiple_of(i * SUB, SUB), SUB)
 
-    gather("plane_recv")
     with jax.named_scope("plane_recv"):
         for i in range(1, NP):
             arrive(pr1.at[lax.rem(p + NP - i, NP)], p1r.at[i])
-        gather("plane_sum")
         total = pr1[0].astype(F32)
         for i in range(1, NP):
             total = total + pr1[i].astype(F32)
@@ -270,15 +281,10 @@
             send(zt.at[sub_rows(to)], za.at[z], p2s.at[i], p2r.at[i], seq=to * NP + p)
         za[z] = zt[sub_rows(z), :]
 
-    gather("intra_b")
-    with jax.named_scope("intra_b"):
-        lax.fori_loop(SPLIT, HEADS, one_intra, 0)
-
     gather("z_scan")
     with jax.named_scope("z_scan"):
         for i in range(1, NZ):
             arrive(za.at[lax.rem(z + NZ - i, NZ)], p2r.at[i])
-        gather("z_sum")
         run = jnp.zeros((SUB, HD), F32)
         for i in range(NZ):
             zb[i] = run
@@ -288,16 +294,10 @@
             send(zb.at[to], zp.at[sub_rows(z)], p3s.at[i], p3r.at[i], seq=to * NP + p)
         zp[sub_rows(z), :] = zb[z]
 
-    gather("gate")
-    with jax.named_scope("gate"):
-        loads[4].wait()
-        lax.fori_loop(0, HEADS, one_gate, 0)
-
     gather("z_back")
     with jax.named_scope("z_back"):
         for i in range(1, NZ):
             arrive(zp.at[sub_rows(lax.rem(z + NZ - i, NZ))], p3r.at[i])
-        gather("back_sum")
         run = zp[...]
         for i in range(NP):
             pr3[i] = run.astype(BF16)
@@ -312,38 +312,46 @@
         for i in range(1, NP):
             arrive(sin.at[piece_rows(lax.rem(p + NP - i, NP))], p4r.at[i])
 
-    def one_head(i, carry):
-        cols = pl.ds(pl.multiple_of(i * HD, HD), HD)
-        att = intra[:, cols] + jnp.dot(qb[:, cols], sin[cols, :], preferred_element_type=F32)
-        ms = jnp.mean(att * att, axis=-1, keepdims=True)
-        nrm[:, cols] = (att * lax.rsqrt(ms + 1e-06) * gate[:, cols]).astype(BF16)
+    ones = jnp.full((HD, HD), 1.0 / HD, BF16)
+
+    GROUP = 6
+
+    def some_heads(i, carry):
+        cols = [pl.ds(pl.multiple_of((i * GROUP + k) * HD, HD), HD) for k in range(GROUP)]
+        att = [intra[:, cl] + jnp.dot(qb[:, cl], sin[cl, :], preferred_element_type=F32) for cl in cols]
+        ms = [jnp.dot((a * a).astype(BF16), ones, preferred_element_type=F32) for a in att]
+        for cl, a, m in zip(cols, att, ms):
+            nrm[:, cl] = (a * lax.rsqrt(m + 1e-06) * gate[:, cl]).astype(BF16)
         return carry
 
+    gather("attend_a")
+    with jax.named_scope("attend"):
+        lax.fori_loop(0, HEADS // GROUP // 2, some_heads, 0)
     gather("attend")
     with jax.named_scope("attend"):
-        lax.fori_loop(0, HEADS, one_head, 0)
+        lax.fori_loop(HEADS // GROUP // 2, HEADS // GROUP, some_heads, 0)
 
     def q_rows(i):
         return pl.ds(pl.multiple_of(i * QT, QT), QT)
 
     def project(n):
         w = wt[plane(ORDER[n // PARTS]), pl.ds(n % PARTS * (NX // PARTS), NX // PARTS)].reshape(CW, WID)
-        pf[n % 3] = lax.dot_general(nrm[...], w, NT, preferred_element_type=F32)
+        pf[n % SLOTS] = lax.dot_general(nrm[...], w, NT, preferred_element_type=F32)
 
     def half_rows(i, half):
         return pl.ds(pl.multiple_of(i * QT + half * QH, QH), QH)
 
     def rs_first(n):
         for half, to in ((0, hu), (1, hd)):
-            t1[n, half] = pf[n % 3, half_rows(h2, half), :].astype(BF16)
+            t1[n, half] = pf[n % SLOTS, half_rows(h2, half), :].astype(BF16)
             send(t1.at[n, half], r1.at[n, half], ys.at[n, half], yr.at[n, half], head=to)
 
     def rs_second(n):
         for half, to in ((0, hu), (1, hd)):
             same, other = pl.ds(half * QH, QH), pl.ds((1 - half) * QH, QH)
-            t2[n, half, other, :] = pf[n % 3, half_rows(to, 1 - half), :].astype(BF16)
+            t2[n, half, other, :] = pf[n % SLOTS, half_rows(to, 1 - half), :].astype(BF16)
             arrive(r1.at[n, half], yr.at[n, half])
-            t2[n, half, same, :] = (pf[n % 3, half_rows(to, half), :] + r1[n, half].astype(F32)).astype(BF16)
+            t2[n, half, same, :] = (pf[n % SLOTS, half_rows(to, half), :] + r1[n, half].astype(F32)).astype(BF16)
             send(t2.at[n, half], r2.at[n, half], ys.at[n, 2 + half], yr.at[n, 2 + half], head=to)
 
     outs = []
@@ -351,15 +359,15 @@
     def rs_last(n):
         arrive(r2.at[n, 0], yr.at[n, 2])
         arrive(r2.at[n, 1], yr.at[n, 3])
-        ob[n] = (pf[n % 3, q_rows(h), :] + r2[n, 0].astype(F32) + r2[n, 1].astype(F32)).astype(BF16)
+        ob[n] = (pf[n % SLOTS, q_rows(h), :] + r2[n, 0].astype(F32) + r2[n, 1].astype(F32)).astype(BF16)
         first = plane(ORDER[n // PARTS]) * PLANE + n % PARTS * CW
         cp = pltpu.make_async_copy(ob.at[n], o_hbm.at[:, pl.ds(pl.multiple_of(first, CW), CW)], out_sem.at[n])
         cp.start()
         outs.append(cp)
 
     marks = [0]
-    for n in range(NCH + 2):
-        gather(f"chunk_{n}")
+    for n in range(NCH + LAG3):
+        gather(f"project_{n}")
         if n < NCH:
             if n % PARTS == 0:
                 with jax.named_scope(f"plane_wait_{n}"):
@@ -367,28 +375,43 @@
             with jax.named_scope(f"project_{n}"):
                 project(n)
                 rs_first(n)
-        if 1 <= n <= NCH:
+        gather(f"reduce_{n}")
+        if LAG2 <= n < NCH + LAG2:
             with jax.named_scope(f"reduce_{n}"):
-                rs_second(n - 1)
-        gather(f"after_{n}")
-        if n >= 2:
+                rs_second(n - LAG2)
+        gather(f"finish_{n}")
+        if n >= LAG3:
             with jax.named_scope(f"finish_{n}"):
-                for cp in sends[marks[max(0, n - 5)] : marks[max(0, n - 4)]]:
+                for cp in sends[marks[max(0, n - LAG3 - 1)] : marks[n - LAG3]]:
                     cp.wait_send()
-                rs_last(n - 2)
+                rs_last(n - LAG3)
         marks.append(len(sends))
 
     with jax.named_scope("drain"):
         for cp in outs:
             cp.wait()
-        for cp in sends[marks[max(0, NCH + 1 - 4)] :]:
+        for cp in sends[marks[NCH - 1] :]:
             cp.wait_send()
+
+
+def land(src, dst, held, sem):
+    rows = QT // 4
+    parts = [pl.ds(i * rows, rows) for i in range(4)]
+    into = [pltpu.make_async_copy(src.at[r], held.at[r], sem.at[0, i]) for i, r in enumerate(parts)]
+    out = [pltpu.make_async_copy(held.at[r], dst.at[r], sem.at[1, i]) for i, r in enumerate(parts)]
+    for cp in into:
+        cp.start()
+    for a, b in zip(into, out):
+        a.wait()
+        b.start()
+    for cp in out:
+        cp.wait()
 
 
 def per_device(queries, key_rows, values, gate_input, norm_gain, out_weight):
     anyspec = pl.BlockSpec(memory_space=pl.ANY)
     dma = lambda *n: pltpu.SemaphoreType.DMA(n)
-    return pl.pallas_call(
+    out = pl.pallas_call(
         kernel,
         out_shape=jax.ShapeDtypeStruct((QT, D), BF16),
         in_specs=[anyspec] * 4 + [pl.BlockSpec(memory_space=pltpu.VMEM), anyspec],
@@ -410,15 +433,15 @@
             pltpu.VMEM((NZ, SUB, HD), F32),
             pltpu.VMEM((NZ, SUB, HD), F32),
             pltpu.VMEM((PIECE, HD), F32),
-            pltpu.VMEM((3, TOK, CW), F32),
+            pltpu.VMEM((SLOTS, TOK, CW), F32),
             pltpu.VMEM((NCH, 2, QH, CW), BF16),
             pltpu.VMEM((NCH, 2, QT, CW), BF16),
             pltpu.VMEM((NCH, 2, QH, CW), BF16),
             pltpu.VMEM((NCH, 2, QT, CW), BF16),
             pltpu.VMEM((NCH, QT, CW), BF16),
             dma(5), dma(NCH),
-            dma(9), dma(9),
-            dma(NZ, 4), dma(NZ, 4),
+            dma(NZ, 2), dma(NZ, 2),
+            dma(NZ, 6), dma(NZ, 6),
             dma(9, NX), dma(9, NX),
             dma(NZ, NX), dma(NZ, NX),
             dma(NP), dma(NP), dma(NZ), dma(NZ), dma(NZ), dma(NZ), dma(NP), dma(NP),
@@ -428,6 +451,13 @@
             collective_id=0, has_side_effects=True, vmem_limit_bytes=60 * 1024 * 1024
         ),
     )(queries, key_rows, values, gate_input, norm_gain, out_weight.T)
+    return pl.pallas_call(
+        land,
+        out_shape=jax.ShapeDtypeStruct((QT, D), BF16),
+        in_specs=[anyspec],
+        out_specs=anyspec,
+        scratch_shapes=[pltpu.VMEM((QT, D), BF16), dma(2, 4)],
+    )(out)
 
 
 def solution(mesh):

time: 112 us -> 107 us (0.955)
  the two profiles are of different devices: /device:TPU:104 before, /device:TPU:1 now
where the time goes in v3:
time: 107 us
  Pallas kernels  106 us (99%)
    pallas_call x1, Pallas kernels, per_device(): pl.pallas_call(kernel, out_shape=jax.ShapeDtypeStruct((QT, D), BF16), in_...  104 us
    pallas_call x1, Pallas kernels, per_device(): pl.pallas_call(land, out_shape=jax.ShapeDtypeStruct((QT, D), BF16), in_sp...  2.2 us

profile of v3, /device:TPU:1, one launch (start us, length us, event | category | flops | bytes accessed | tf_op | source)
XLA Modules:
  0.0 106.6 jit_solution(5901590797972786180)
XLA Ops:
  0.0 104.2 %shard_map.64.src = bf16[128,6144]{1,0:T(8,128)(2,1)} custom-call(bf16[512,1536]{1,0:T(8,128)(2,1)} %q_hbm.1, bf16[512,1536]{1,0:T(8,128)(2,1)} %k_hbm.1, bf16[512,1536]{1,0:T(8,128)(2,1)} %v_hbm.1, bf16[512,1536]{1,0:T(8,128)(2,1)} %g_hbm.1, f32[1536]{0:T(1024)} %gain_ref.1, bf16[96,1536]{1,0:T(8,128)(2,1)} %bitcast.1), custom_call_target="tpu_custom_call" | custom-call | tf_op jit(solution)/shard_map/pallas_call | solution.py:414
  104.2 2.2 %shard_map.65 = bf16[128,6144]{1,0:T(8,128)(2,1)} custom-call(bf16[128,6144]{1,0:T(8,128)(2,1)} %shard_map.64.src), custom_call_target="tpu_custom_call" | custom-call | tf_op jit(solution)/shard_map/pallas_call | solution.py:454

commit v4 on v3

--- a/solution.py
+++ b/solution.py
@@ -23,6 +23,8 @@
 LAG2, LAG3 = 2, 4
 SLOTS = LAG3 + 1
 PARTS = 2
+FAR_X = (4, 5, 2, 6, 3, 7, 1)
+FAR_Z = (4, 3, 5, 2, 6, 1, 7)
 NCH = NZ * PARTS
 CW = PLANE // PARTS
 QH = QT // 2
@@ -30,25 +32,25 @@
 KINDS = "BAABBBBB"
 ORDER = (0, 4, 1, 2, 6, 3, 5, 7)
 PLAN = {
-    "plane_recv": "O0 I0 Z4 X0",
-    "z_scan": "Z2 I2 Z5 G0 Z3 F0 I3 Z8",
-    "z_back": "Z9 X4 S0 A0 Z7",
-    "state_recv": "Z6 Z12 Z13 I1 F4 X6",
-    "project_1": "S4",
-    "reduce_2": "X3",
-    "reduce_3": "S1",
-    "reduce_4": "S2 F6",
-    "reduce_5": "F3",
-    "project_6": "Z11",
-    "reduce_6": "Z10",
-    "project_7": "X5",
-    "reduce_7": "S6 S3",
-    "finish_8": "F5",
-    "project_9": "Z14",
-    "project_10": "X7",
-    "finish_10": "S5",
-    "project_12": "F7",
-    "finish_13": "S7",
+    "plane_recv": ("O0", "I0", "Z4", "X0", "X1",),
+    "z_scan": ("Z2", "I2", "Z5", "G0", "Z3", "F0", "I3", "Z8",),
+    "z_back": ("Z9", "X8", "X9", "S0", "A1", "A2", "A3", "Z7",),
+    "state_recv": ("Z6", "Z12", "Z13", "I1", "F4", "X12", "X13",),
+    "project_1": ("S4",),
+    "reduce_2": ("X6", "X7",),
+    "reduce_3": ("S1",),
+    "reduce_4": ("S2", "F6",),
+    "reduce_5": ("F3",),
+    "project_6": ("Z11",),
+    "reduce_6": ("Z10",),
+    "project_7": ("X10", "X11",),
+    "reduce_7": ("S6", "S3",),
+    "finish_8": ("F5",),
+    "project_9": ("Z14",),
+    "project_10": ("X14", "X15",),
+    "finish_10": ("S5",),
+    "project_12": ("F7",),
+    "finish_13": ("S7",),
 }
 NT = (((1,), (1,)), ((), ()))
 TN = (((0,), (0,)), ((), ()))
@@ -145,13 +147,13 @@
         ref = shard(plane(j), lax.rem(x + i, NX), c)
         send(ref, ref, ss.at[j, i], sr.at[j, i], seq=dev_sib)
 
-    def x_start(j):
+    def x_start(j, i):
         ref = shard(plane(j), x, c)
-        for i in range(2):
-            up, dn = part(ref, i), part(ref, 1 - i)
-            send(up, up, xs.at[j, i], xr.at[j, i], seq=dev_xu)
-            send(dn, dn, xs.at[j, 2 + i], xr.at[j, 2 + i], seq=dev_xd)
-        sib_send(j, 0)
+        up, dn = part(ref, i), part(ref, 1 - i)
+        send(up, up, xs.at[j, i], xr.at[j, i], seq=dev_xu)
+        send(dn, dn, xs.at[j, 2 + i], xr.at[j, 2 + i], seq=dev_xd)
+        if i == 0:
+            sib_send(j, 0)
 
     def x_forward(j):
         pln = plane(j)
@@ -165,15 +167,14 @@
     def halves(ref):
         return part(ref, 0), part(ref, 1)
 
-    def whole_start(j):
-        for i in range(1, NX):
-            ref = shard(plane(j), lax.rem(x + i, NX), c)
-            if j % 2 or j == 0:
-                up = halves(ref)[0] if j == 5 else ref
-                send(up, up, fs.at[j + 2 - (j == 0), i], fr.at[j + 2 - (j == 0), i], seq=dev_zu)
-            if j % 2 == 0:
-                dn = halves(ref)[1] if j == 6 else ref
-                send(dn, dn, fs.at[j + 2, i], fr.at[j + 2, i], seq=dev_zd)
+    def whole_start(j, i):
+        ref = shard(plane(j), lax.rem(x + i, NX), c)
+        if j % 2 or j == 0:
+            up = part(ref, 0) if j == 5 else ref
+            send(up, up, fs.at[j + 2 - (j == 0), i], fr.at[j + 2 - (j == 0), i], seq=dev_zu)
+        if j % 2 == 0:
+            dn = part(ref, 1) if j == 6 else ref
+            send(dn, dn, fs.at[j + 2, i], fr.at[j + 2, i], seq=dev_zd)
 
     def fill(j):
         pln = plane(j)
@@ -202,10 +203,10 @@
         for i in range(NX):
             arrive(shard(plane(j), lax.rem(x + i, NX), 1 - c), sr.at[j, i])
 
-    stages = {"O": lambda j: z_start(), "Z": lambda j: z_recv(j // 2, j % 2), "X": x_start, "F": x_forward, "A": whole_start, "S": fill}
+    stages = {"O": lambda j: z_start(), "Z": lambda j: z_recv(j // 2, j % 2), "X": lambda j: x_start(j // 2, j % 2), "F": x_forward, "A": lambda j: whole_start(j // 4, j % 4), "S": fill}
 
     def gather(at):
-        for name in PLAN.get(at, "").split():
+        for name in PLAN.get(at, ()):
             with jax.named_scope(f"gather_{name}"):
                 stages[name[0]](int(name[1:]))
 
@@ -223,12 +224,15 @@
     with jax.named_scope("entry_barrier"):
         pl.semaphore_wait(bar, NP - 1 + NZ - 1 + 2)
 
+    def mate(i, way=1):
+        return lax.rem(x + NX + way * (i // NC), NX) * NC + lax.rem(c + i, NC)
+
     def piece_rows(i):
         return pl.ds(pl.multiple_of(i * PIECE, PIECE), PIECE)
 
     with jax.named_scope("plane_send"):
-        for i in range(1, NP):
-            to = lax.rem(p + i, NP)
+        for i in FAR_X:
+            to = mate(i)
             send(st.at[piece_rows(to)], pr1.at[p], p1s.at[i], p1r.at[i], seq=z * NP + to)
         pr1[p] = st[piece_rows(p), :]
 
@@ -270,47 +274,47 @@
         return pl.ds(pl.multiple_of(i * SUB, SUB), SUB)
 
     with jax.named_scope("plane_recv"):
-        for i in range(1, NP):
-            arrive(pr1.at[lax.rem(p + NP - i, NP)], p1r.at[i])
+        for i in FAR_X:
+            arrive(pr1.at[mate(i, -1)], p1r.at[i])
         total = pr1[0].astype(F32)
         for i in range(1, NP):
             total = total + pr1[i].astype(F32)
         zt[...] = total
-        for i in range(1, NZ):
+        for i in FAR_Z:
             to = lax.rem(z + i, NZ)
             send(zt.at[sub_rows(to)], za.at[z], p2s.at[i], p2r.at[i], seq=to * NP + p)
         za[z] = zt[sub_rows(z), :]
 
     gather("z_scan")
     with jax.named_scope("z_scan"):
-        for i in range(1, NZ):
+        for i in FAR_Z:
             arrive(za.at[lax.rem(z + NZ - i, NZ)], p2r.at[i])
         run = jnp.zeros((SUB, HD), F32)
         for i in range(NZ):
             zb[i] = run
             run = run + za[i]
-        for i in range(1, NZ):
+        for i in FAR_Z:
             to = lax.rem(z + i, NZ)
             send(zb.at[to], zp.at[sub_rows(z)], p3s.at[i], p3r.at[i], seq=to * NP + p)
         zp[sub_rows(z), :] = zb[z]
 
     gather("z_back")
     with jax.named_scope("z_back"):
-        for i in range(1, NZ):
+        for i in FAR_Z:
             arrive(zp.at[sub_rows(lax.rem(z + NZ - i, NZ))], p3r.at[i])
         run = zp[...]
         for i in range(NP):
             pr3[i] = run.astype(BF16)
             run = run + pr1[i].astype(F32)
-        for i in range(1, NP):
-            to = lax.rem(p + i, NP)
+        for i in FAR_X:
+            to = mate(i)
             send(pr3.at[to], sin.at[piece_rows(p)], p4s.at[i], p4r.at[i], seq=z * NP + to)
         sin[piece_rows(p), :] = pr3[p]
 
     gather("state_recv")
     with jax.named_scope("state_recv"):
-        for i in range(1, NP):
-            arrive(sin.at[piece_rows(lax.rem(p + NP - i, NP))], p4r.at[i])
+        for i in FAR_X:
+            arrive(sin.at[piece_rows(mate(i, -1))], p4r.at[i])
 
     ones = jnp.full((HD, HD), 1.0 / HD, BF16)
 

time: 107 us -> 106 us (level)
  no operation moved by 1% of the time
where the time goes in v4:
time: 106 us
  Pallas kernels  106 us (100%)
    pallas_call x1, Pallas kernels, per_device(): pl.pallas_call(kernel, out_shape=jax.ShapeDtypeStruct((QT, D), BF16), in_...  104 us
    pallas_call x1, Pallas kernels, per_device(): pl.pallas_call(land, out_shape=jax.ShapeDtypeStruct((QT, D), BF16), in_sp...  2.2 us

profile of v4, /device:TPU:1, one launch (start us, length us, event | category | flops | bytes accessed | tf_op | source)
XLA Modules:
  0.0 106.0 jit_solution(9249679063861436521)
XLA Ops:
  0.0 103.6 %shard_map.64.src = bf16[128,6144]{1,0:T(8,128)(2,1)} custom-call(bf16[512,1536]{1,0:T(8,128)(2,1)} %q_hbm.1, bf16[512,1536]{1,0:T(8,128)(2,1)} %k_hbm.1, bf16[512,1536]{1,0:T(8,128)(2,1)} %v_hbm.1, bf16[512,1536]{1,0:T(8,128)(2,1)} %g_hbm.1, f32[1536]{0:T(1024)} %gain_ref.1, bf16[96,1536]{1,0:T(8,128)(2,1)} %bitcast.1), custom_call_target="tpu_custom_call" | custom-call | tf_op jit(solution)/shard_map/pallas_call | solution.py:418
  103.7 2.2 %shard_map.65 = bf16[128,6144]{1,0:T(8,128)(2,1)} custom-call(bf16[128,6144]{1,0:T(8,128)(2,1)} %shard_map.64.src), custom_call_target="tpu_custom_call" | custom-call | tf_op jit(solution)/shard_map/pallas_call | solution.py:458

commit v5 on v4

--- a/solution.py
+++ b/solution.py
@@ -257,17 +257,18 @@
         for cl, a, d in zip(cols, full, diag):
             intra[hi, cl] = jnp.dot(a, vb[lo, cl], preferred_element_type=F32) + jnp.dot(d, vb[hi, cl], preferred_element_type=F32)
 
-    def one_gate(i, carry):
-        cols = pl.ds(pl.multiple_of(i * HD, HD), HD)
-        gi = gb[:, cols].astype(F32)
-        gate[:, cols] = gi / (1.0 + jnp.exp(-gi)) * gain_ref[cols].reshape(1, HD)
+    def some_gates(i, carry):
+        for k in range(3):
+            cols = pl.ds(pl.multiple_of((3 * i + k) * HD, HD), HD)
+            gi = gb[:, cols].astype(F32)
+            gate[:, cols] = gi / (1.0 + jnp.exp(-gi)) * gain_ref[cols].reshape(1, HD)
         return carry
 
     def intra_part(i):
         some_intra(3 * i)
 
     stages["I"] = intra_part
-    stages["G"] = lambda j: lax.fori_loop(0, HEADS, one_gate, 0)
+    stages["G"] = lambda j: lax.fori_loop(0, HEADS // 3, some_gates, 0)
     gather("plane_recv")
 
     def sub_rows(i):
@@ -399,8 +400,8 @@
 
 
 def land(src, dst, held, sem):
-    rows = QT // 4
-    parts = [pl.ds(i * rows, rows) for i in range(4)]
+    rows = QT // 8
+    parts = [pl.ds(i * rows, rows) for i in range(8)]
     into = [pltpu.make_async_copy(src.at[r], held.at[r], sem.at[0, i]) for i, r in enumerate(parts)]
     out = [pltpu.make_async_copy(held.at[r], dst.at[r], sem.at[1, i]) for i, r in enumerate(parts)]
     for cp in into:
@@ -460,7 +461,7 @@
         out_shape=jax.ShapeDtypeStruct((QT, D), BF16),
         in_specs=[anyspec],
         out_specs=anyspec,
-        scratch_shapes=[pltpu.VMEM((QT, D), BF16), dma(2, 4)],
+        scratch_shapes=[pltpu.VMEM((QT, D), BF16), dma(2, 8)],
     )(out)
 
 

time: 106 us -> 106 us (level)
  no operation moved by 1% of the time
where the time goes in v5:
time: 106 us
  Pallas kernels  106 us (100%)
    pallas_call x1, Pallas kernels, per_device(): pl.pallas_call(kernel, out_shape=jax.ShapeDtypeStruct((QT, D), BF16), in_...  104 us
    pallas_call x1, Pallas kernels, per_device(): pl.pallas_call(land, out_shape=jax.ShapeDtypeStruct((QT, D), BF16), in_sp...  2.29 us

profile of v5, /device:TPU:1, one launch (start us, length us, event | category | flops | bytes accessed | tf_op | source)
XLA Modules:
  0.0 106.1 jit_solution(7823253078115278216)
XLA Ops:
  0.0 103.6 %shard_map.64.src = bf16[128,6144]{1,0:T(8,128)(2,1)} custom-call(bf16[512,1536]{1,0:T(8,128)(2,1)} %q_hbm.1, bf16[512,1536]{1,0:T(8,128)(2,1)} %k_hbm.1, bf16[512,1536]{1,0:T(8,128)(2,1)} %v_hbm.1, bf16[512,1536]{1,0:T(8,128)(2,1)} %g_hbm.1, f32[1536]{0:T(1024)} %gain_ref.1, bf16[96,1536]{1,0:T(8,128)(2,1)} %bitcast.1), custom_call_target="tpu_custom_call" | custom-call | tf_op jit(solution)/shard_map/pallas_call | solution.py:419
  103.7 2.3 %shard_map.65 = bf16[128,6144]{1,0:T(8,128)(2,1)} custom-call(bf16[128,6144]{1,0:T(8,128)(2,1)} %shard_map.64.src), custom_call_target="tpu_custom_call" | custom-call | tf_op jit(solution)/shard_map/pallas_call | solution.py:459
